TPU v7x, 32 devices: a whole 2x2x4 slice. The times are simulated.
32 devices in a mesh: groups: 1, node: 2 (over core), local: 16 (over z, y, x).
Axes of the slice: x: 2, y: 2, z: 4, core: 2. Of those that a mesh axis runs over, the one named last changes fastest.
Arguments:
- tokens: bfloat16 [2048, 3584], P(('groups', 'local'), 'node'), may hold values from -6 to 6
- expert_ids: int32 [2048, 8], P(('groups', 'local')), may hold values from 0 to 15, all different within a row; in each aligned block of 128 rows (0 to 127, 128 to 255, ...) at most 80 rows name the same one
- gate_probs: float32 [2048, 8], P(('groups', 'local')), may hold values from 0.05 to 1
- w_gate: bfloat16 [16, 3584, 1024], P('local', 'node'), may hold values from -0.09375 to 0.09375
- w_up: bfloat16 [16, 3584, 1024], P('local', 'node'), may hold values from -0.09375 to 0.09375
- w_down: bfloat16 [16, 1024, 3584], P('local', 'node'), may hold values from -0.1875 to 0.1875
- gate_scale: float32 [16, 1024], P('local', 'node'), may hold values from 0.5 to 2
- up_scale: float32 [16, 1024], P('local', 'node'), may hold values from 0.5 to 2
- down_scale: float32 [16, 3584], P('local'), may hold values from 0.5 to 2
- cotangent: bfloat16 [2048, 3584], P(('groups', 'local'), 'node'), may hold values from -0.19921875 to 0.19921875
Outputs:
- mixed: bfloat16 [2048, 3584], P(('groups', 'local'), 'node')
- gate_grad: float32 [2048, 8], P(('groups', 'local'))
Inputs may be any that keep to these rules, and one draw needn't show every extreme that they name: `expert_ids`: each token names 8 different experts; among the tokens of one block of 128 no expert is named more than 80 times, and in every draw some expert is named exactly 80 times in some block.
All inputs are finite; a program needn't handle non-finite values.
Results may differ from a plain program's by a relative error of at most 0.018.
Values may be sent and summed in bfloat16 or wider, within the bound.
A program may use at most 128 MiB of HBM per device.

v0:
```python
import jax
import jax.numpy as jnp
from jax import lax
from jax.sharding import PartitionSpec as P


def on_device(
    tokens,
    expert_ids,
    gate_probs,
    w_gate,
    w_up,
    w_down,
    gate_scale,
    up_scale,
    down_scale,
    cotangent,
):
    experts = lax.axis_size("local")
    tok_rows, top_count = expert_ids.shape
    capacity = max(2, min(tok_rows, tok_rows * top_count * 5 // (4 * experts)))
    pair_count = tok_rows * top_count
    chosen = expert_ids.reshape(pair_count)
    onehot = (chosen[:, None] == jnp.arange(experts, dtype=jnp.int32)[None, :]).astype(jnp.int32)
    earlier = jnp.cumsum(onehot, axis=0) - onehot
    position = jnp.sum(earlier * onehot, axis=1)
    target = chosen * capacity + position
    owning = jnp.arange(pair_count, dtype=jnp.int32) // top_count
    features = tokens.shape[1]
    outgoing = (
        jnp.zeros((experts * capacity, features), jnp.bfloat16).at[target].set(tokens[owning])
    )
    outgoing = outgoing.reshape(experts, capacity, features)
    received = lax.all_to_all(outgoing, "local", split_axis=0, concat_axis=0, tiled=True)
    sources, slot_count, widths = received.shape
    slot_rows = received.reshape(sources * slot_count, widths)
    gate_part = jnp.dot(slot_rows, w_gate[0], preferred_element_type=jnp.float32)
    up_part = jnp.dot(slot_rows, w_up[0], preferred_element_type=jnp.float32)
    gate_sum = lax.psum_scatter(
        gate_part.astype(jnp.bfloat16), "node", scatter_dimension=1, tiled=True
    ).astype(jnp.float32)
    up_sum = lax.psum_scatter(
        up_part.astype(jnp.bfloat16), "node", scatter_dimension=1, tiled=True
    ).astype(jnp.float32)
    hidden = (jax.nn.silu(gate_sum * gate_scale[0]) * (up_sum * up_scale[0])).astype(jnp.bfloat16)
    partial_value = jnp.dot(hidden, w_down[0], preferred_element_type=jnp.float32) * down_scale[0]
    summed = lax.psum_scatter(
        partial_value.astype(jnp.bfloat16), "node", scatter_dimension=1, tiled=True
    )
    returned = lax.all_to_all(
        summed.reshape(sources, slot_count, -1), "local", split_axis=0, concat_axis=0, tiled=True
    )
    picked = returned.reshape(experts * capacity, features)[target].reshape(
        tok_rows, top_count, features
    )
    combined = jnp.sum(picked.astype(jnp.float32) * gate_probs[:, :, None], axis=1).astype(
        jnp.bfloat16
    )
    local_dots = jnp.einsum("tkf,tf->tk", picked, cotangent, preferred_element_type=jnp.float32)
    gate_grad = lax.psum(local_dots, "node")
    return (combined, gate_grad)


def solution(mesh):
    return jax.shard_map(
        on_device,
        mesh=mesh,
        in_specs=(
            P(("groups", "local"), "node"),
            P(("groups", "local"), None),
            P(("groups", "local"), None),
            P("local", "node", None),
            P("local", "node", None),
            P("local", "node", None),
            P("local", "node"),
            P("local", "node"),
            P("local", None),
            P(("groups", "local"), "node"),
        ),
        out_specs=(P(("groups", "local"), "node"), P(("groups", "local"), None)),
        check_vma=False,
    )
```

profile of v0, /device:TPU:15, one launch (start us, length us, event | category | flops | bytes accessed | tf_op | source)
XLA Modules:
  0.0 345.9 jit_solution(10779611450971039449)
XLA Ops:
  7.2 0.0 copy-start
  7.2 0.0 reduce-scatter.4.cloned.1.call-start
  7.2 0.8 copy.16
  8.1 0.1 eq.29
  8.2 0.1 eq.25
  8.2 0.7 broadcast_multiply_fusion
  9.0 4.5 %reduce-window.6 = s32[16,8,128]{2,1,0:T(8,128)S(1)} reduce-window(s32[16,8,128]{2,1,0:T(8,128)S(1)} %fusion.16, s32[]{:T(128)} %constant.28.clone.1), window={size=1x1x128 pad=0_0x0_0x127_0}, to_apply=%region_0.0 | reduce-window | flops 2080768 | bytes 131076 | tf_op jit(solution)/shard_map/reduce-window
  13.5 0.1 slice.12
  13.6 0.1 copy.18
  13.7 0.1 copy.19
  13.8 0.1 broadcast_add_fusion
  13.9 0.1 copy.15
  14.0 0.1 mul.66
  14.2 0.0 copy-done
  14.2 20.6 %scatter_custom_fusion = bf16[1280,1792]{1,0:T(8,128)(2,1)} fusion(s32[1024]{0:T(1024)S(1)} %bitcast.51, bf16[128,1792]{1,0:T(8,128)(2,1)S(1)} %copy-done, s32[1024]{0:T(1024)S(1)} %broadcast_clamp_fusion.1, bf16[]{:T(256)} %constant.26.clone.1), kind=kCustom, calls=%fused_computation.13 | custom fusion | bytes 4587522 | tf_op jit(solution)/shard_map/scatter | solution.py:31
  34.7 0.0 copy-start.5
  34.7 106.7 %all_to_all.10 = bf16[16,80,1792]{2,1,0:T(8,128)(2,1)S(1)} all-to-all(bf16[16,80,1792]{2,1,0:T(8,128)(2,1)} %bitcast.44), channel_id=1, replica_groups=mesh['groups'=1,'node'=2,'local'=16] {'local'}, dimensions={0} | all-to-all | bytes 9175040 | tf_op jit(solution)/shard_map/all_to_all | solution.py:34
  141.4 0.0 copy-start.2
  141.4 2.0 copy-done.2
  143.5 0.0 copy-done.5
  143.5 6.1 %convolution_convert_fusion.1 = bf16[1280,1024]{1,0:T(8,128)(2,1)} fusion(bf16[1280,1792]{1,0:T(8,128)(2,1)S(1)} %bitcast.46, bf16[1,1792,1024]{2,1,0:T(8,128)(2,1)S(1)} %copy-done.5), kind=kOutput, calls=%fused_computation.7 | convolution fusion | flops 4698931200 | bytes 10878976 | tf_op jit(solution)/shard_map/dot_general | solution.py:37
  149.6 0.0 reduce-scatter.4.cloned.1.call-update
  149.7 0.0 copy-start.3
  149.7 0.0 copy-start.7
  149.7 0.0 copy-start.8
  149.7 0.0 reduce-scatter.6.cloned.1.call-start
  149.8 9.9 %convolution_convert_fusion = bf16[1280,1024]{1,0:T(8,128)(2,1)} fusion(bf16[1280,1792]{1,0:T(8,128)(2,1)} %bitcast.47, bf16[1,1792,1024]{2,1,0:T(8,128)(2,1)} %param.14), kind=kOutput, calls=%fused_computation.6 | convolution fusion | flops 4698931200 | bytes 10878976 | tf_op jit(solution)/shard_map/dot_general | solution.py:38
  159.7 0.0 reduce-scatter.6.cloned.1.call-update
  159.7 0.0 reduce-scatter.8.cloned.1.call-start
  159.7 0.0 copy-done.3
  159.8 1.7 reduce-scatter.4.cloned.1.call-done
  161.5 13.8 %reduce-scatter.6.cloned.1.call-done = bf16[1280,512]{1,0:T(8,128)(2,1)} async-done(((bf16[1280,1024]{1,0:T(8,128)(2,1)}), bf16[1280,512]{1,0:T(8,128)(2,1)}) %reduce-scatter.6.cloned.1.call-update) | async-done | bytes 1310736 | tf_op jit(solution)/shard_map/reduce_scatter | solution.py:42
  175.3 0.0 copy-done.7
  175.3 0.0 copy-done.8
  175.3 11.7 %fusion = bf16[1280,3584]{1,0:T(8,128)(2,1)} fusion(f32[3584]{0:T(1024)S(1)} %reduce, bf16[1,512,3584]{2,1,0:T(8,128)(2,1)} %param.15, bf16[1280,512]{1,0:T(8,128)(2,1)} %reduce-scatter.6.cloned.1.call-done, bf16[1280,512]{1,0:T(8,128)(2,1)} %reduce-scatter.4.cloned.1.call-done, f32[512]{0:T(512)S(1)} %bitcast.56, f32[512]{0:T(512)S(1)} %bitcast.57), kind=kOutput, calls=%fused_computation.4 | convolution fusion | flops 4713349120 | bytes 15484928 | tf_op jit(solution)/shard_map/dot_general | solution.py:46
  186.9 0.0 reduce-scatter.8.cloned.1.call-update
  187.0 18.9 %reduce-scatter.8.cloned.1.call-done = bf16[1280,1792]{1,0:T(8,128)(2,1)} async-done(((bf16[1280,3584]{1,0:T(8,128)(2,1)}), bf16[1280,1792]{1,0:T(8,128)(2,1)}) %reduce-scatter.8.cloned.1.call-update) | async-done | bytes 4587536 | tf_op jit(solution)/shard_map/reduce_scatter | solution.py:47
  205.8 0.0 copy-start.4
  205.8 6.5 %all-to-all-start.1 = ((bf16[16,80,1792]{2,1,0:T(8,128)(2,1)}), bf16[16,80,1792]{2,1,0:T(8,128)(2,1)}, u32[]{:S(2)}, u32[]{:S(2)}) async-start(bf16[16,80,1792]{2,1,0:T(8,128)(2,1)} %bitcast.45), calls=%async_computation.4 | async-start | bytes 9175040 | tf_op jit(solution)/shard_map/all_to_all | solution.py:50
  212.4 0.0 copy-done.4
  212.4 0.1 copy.20
  212.5 103.6 %all-to-all-done.1 = bf16[16,80,1792]{2,1,0:T(8,128)(2,1)} async-done(((bf16[16,80,1792]{2,1,0:T(8,128)(2,1)}), bf16[16,80,1792]{2,1,0:T(8,128)(2,1)}, u32[]{:S(2)}, u32[]{:S(2)}) %all-to-all-start.1) | async-done | bytes 4587552 | tf_op jit(solution)/shard_map/all_to_all | solution.py:50
  316.1 10.8 %gather_fusion = bf16[1024,1792]{1,0:T(8,128)(2,1)} fusion(bf16[1280,1792]{1,0:T(8,128)(2,1)} %bitcast.13, s32[1024]{0:T(1024)S(1)} %broadcast_clamp_fusion), kind=kCustom, calls=%fused_computation.1 | custom fusion | bytes 7344128 | tf_op jit(solution)/shard_map/gather | solution.py:53
  326.9 0.0 copy-start.1
  326.9 0.0 copy-start.6
  326.9 6.3 %multiply_reduce_fusion = bf16[128,1792]{1,0:T(8,128)(2,1)} fusion(bf16[1024,1792]{1,0:T(8,128)(2,1)} %gather_fusion, f32[128,8]{1,0:T(8,128)S(1)} %copy.20), kind=kLoop, calls=%fused_computation.5 | loop fusion | flops 5275648 | bytes 4132864 | tf_op jit(solution)/shard_map/reduce_sum | solution.py:56
  333.2 0.0 copy-done.1
  333.2 0.0 copy-done.6
  333.2 2.1 fusion.1
  335.3 0.1 copy.22
  335.3 4.1 %psum.7 = f32[128,8]{0,1:T(8,128)} all-reduce(f32[128,8]{0,1:T(8,128)S(1)} %bitcast.53), channel_id=1, replica_groups=mesh['groups'=1,'node'=2,'local'=16] {'node'}, use_global_device_ids=true, to_apply=%region_8.9 | all-reduce | flops 1024 | bytes 8192 | tf_op jit(solution)/shard_map/psum | solution.py:60
  (9 shorter events, 0.1 us)
Async XLA Ops:
  7.2 7.0 %copy-start = (bf16[128,1792]{1,0:T(8,128)(2,1)S(1)}, bf16[128,1792]{1,0:T(8,128)(2,1)}, u32[]{:S(2)}) copy-start(bf16[128,1792]{1,0:T(8,128)(2,1)} %param.10) | copy-start | bytes 1376260
  7.2 154.3 %reduce-scatter.4.cloned.1.call-start = ((), (), s32[]{:S(2)}) async-start(), calls=%async_computation.5 | async-start | bytes 3932160 | tf_op jit(solution)/shard_map/reduce_scatter | solution.py:39
  34.7 108.8 %copy-start.5 = (bf16[1,1792,1024]{2,1,0:T(8,128)(2,1)S(1)}, bf16[1,1792,1024]{2,1,0:T(8,128)(2,1)}, u32[]{:S(2)}) copy-start(bf16[1,1792,1024]{2,1,0:T(8,128)(2,1)} %param.13) | copy-start | bytes 11010052
  141.4 2.1 copy-start.2
  149.7 10.1 %copy-start.3 = (f32[1,3584]{1,0:T(1,128)S(1)}, f32[1,3584]{1,0:T(1,128)}, u32[]{:S(2)}) copy-start(f32[1,3584]{1,0:T(1,128)} %param.18) | copy-start | bytes 43012
  149.7 25.6 %copy-start.7 = (f32[1,512]{1,0:T(1,128)S(1)}, f32[1,512]{1,0:T(1,128)}, u32[]{:S(2)}) copy-start(f32[1,512]{1,0:T(1,128)} %param.17) | copy-start | bytes 6148
  149.7 25.6 %copy-start.8 = (f32[1,512]{1,0:T(1,128)S(1)}, f32[1,512]{1,0:T(1,128)}, u32[]{:S(2)}) copy-start(f32[1,512]{1,0:T(1,128)} %param.16) | copy-start | bytes 6148
  149.7 25.6 %reduce-scatter.6.cloned.1.call-start = ((), (), s32[]{:S(2)}) async-start(), calls=%async_computation.6 | async-start | bytes 3932160 | tf_op jit(solution)/shard_map/reduce_scatter | solution.py:42
  159.7 46.1 %reduce-scatter.8.cloned.1.call-start = ((), (), s32[]{:S(2)}) async-start(), calls=%async_computation.7 | async-start | bytes 13762560 | tf_op jit(solution)/shard_map/reduce_scatter | solution.py:47
  205.8 6.5 %copy-start.4 = (f32[128,8]{0,1:T(8,128)S(1)}, f32[128,8]{0,1:T(8,128)}, u32[]{:S(2)}) copy-start(f32[128,8]{0,1:T(8,128)} %param.12) | copy-start | bytes 12292
  205.8 110.3 %all-to-all-start.1 = ((bf16[16,80,1792]{2,1,0:T(8,128)(2,1)}), bf16[16,80,1792]{2,1,0:T(8,128)(2,1)}, u32[]{:S(2)}, u32[]{:S(2)}) async-start(bf16[16,80,1792]{2,1,0:T(8,128)(2,1)} %bitcast.45), calls=%async_computation.4 | async-start | bytes 9175040 | tf_op jit(solution)/shard_map/all_to_all | solution.py:50
  326.9 6.3 %copy-start.1 = (bf16[1024,1792]{1,0:T(8,128)(2,1)S(1)}, bf16[1024,1792]{1,0:T(8,128)(2,1)}, u32[]{:S(2)}) copy-start(bf16[1024,1792]{1,0:T(8,128)(2,1)} %gather_fusion) | copy-start | bytes 11010052
  326.9 6.3 %copy-start.6 = (bf16[128,1792]{1,0:T(8,128)(2,1)S(1)}, bf16[128,1792]{1,0:T(8,128)(2,1)}, u32[]{:S(2)}) copy-start(bf16[128,1792]{1,0:T(8,128)(2,1)} %param.19) | copy-start | bytes 1376260
Sparse Core Ops, SparseCore 0:
  149.8 11.6 reduce-scatter.3
  163.8 11.4 reduce-scatter.5
  187.1 18.6 reduce-scatter.7
where the time goes:
time: 346 us
  waiting for transfers between devices  138 us (40%)
  blocking collectives  111 us (32%)
  local copies, waits for them, and re-layouts  35.1 us (10%)
  matrix products  29.8 us (9%)
  between operations  13.9 us (4%)
  other arithmetic  11.7 us (3%)
  starting transfers between devices  6.67 us (2%)
    all_to_all x1, blocking collectives, on_device(): lax.all_to_all(outgoing, 'local', split_axis=0, concat_axis=0, tiled=True)  107 us
    all_to_all x1, waiting for transfers between devices, on_device(): lax.all_to_all(summed.reshape(sources, slot_count, -1), 'local', split_ax...  104 us
    scatter x1, local copies, waits for them, and re-layouts, on_device(): jnp.zeros((experts * capacity, features), jnp.bfloat16).at[target]  20.6 us
    reduce_scatter x1, waiting for transfers between devices, on_device(): lax.psum_scatter(partial_value.astype(jnp.bfloat16), 'node', scatter_dime...  18.9 us
    reduce_scatter x1, waiting for transfers between devices, on_device(): lax.psum_scatter(up_part.astype(jnp.bfloat16), 'node', scatter_dimension=...  13.8 us
    dot_general x1, matrix products, on_device(): jnp.dot(hidden, w_down[0], preferred_element_type=jnp.float32)  11.7 us
    gather x1, local copies, waits for them, and re-layouts, on_device(): returned.reshape(experts * capacity, features)[target]  10.8 us
    dot_general x1, matrix products, on_device(): up_part = jnp.dot(slot_rows, w_up[0], preferred_element_type=jnp.float32)  9.91 us
  transfers between devices with their start and end apart: 4, of which 4 were waited for; matrix products, arithmetic and copies ran while one was open for 3% of the time, Pallas kernels for 0%

commit v1 on v0

--- a/solution.py
+++ b/solution.py
@@ -2,6 +2,13 @@
 import jax.numpy as jnp
 from jax import lax
 from jax.sharding import PartitionSpec as P
+from jax.experimental import pallas as pl
+from jax.experimental.pallas import tpu as pltpu
+
+
+MESH = pl.DeviceIdType.MESH
+BF = jnp.bfloat16
+F32 = jnp.float32
 
 
 def on_device(
@@ -61,9 +68,427 @@
     return (combined, gate_grad)
 
 
+def layer_kernel(
+    tokens, ids, probs, w_gate, w_up, w_down, gate_scale, up_scale, down_scale, cot,
+    mixed, gate_grad,
+    buf, w_mine, w_oth, wd, ds, codes_out, codes_in, code_mat, prob_mat,
+    slots, psend, precv, mine, hid, outb, ret, acc, dots, dots_in,
+    load_sem, own_sem, blk_send, blk_recv, code_send, code_recv,
+    part_send, part_recv, hid_send, hid_recv, ret_send, ret_recv, wd_send, wd_recv,
+    dot_send, dot_recv,
+):
+    experts, cap, width = outb.shape
+    rows = tokens.shape[0]
+    half = rows // 2
+    inner = gate_scale.shape[1]
+    top = ids.shape[1]
+    levels = experts // 4
+    me = lax.axis_index("local")
+    nd = lax.axis_index("node")
+    z, c = me // 4, me % 4
+    y, x = c // 2, c % 2
+    xn, yn = me + 1 - 2 * x, me + 2 - 4 * y
+    other = 1 - nd
+
+    def remote(src, dst, send, recv, where):
+        return pltpu.make_async_remote_copy(
+            src_ref=src, dst_ref=dst, send_sem=send, recv_sem=recv,
+            device_id=where, device_id_type=MESH,
+        )
+
+    my_cols = pl.ds(pl.multiple_of(nd * inner, 128), inner)
+    oth_cols = pl.ds(pl.multiple_of(other * inner, 128), inner)
+    my_feat = pl.ds(pl.multiple_of(nd * width, 128), width)
+    oth_feat = pl.ds(pl.multiple_of(other * width, 128), width)
+    my_rows = pl.ds(pl.multiple_of(nd * inner, 128), inner)
+    loads = [
+        pltpu.make_async_copy(w_gate.at[0, :, oth_cols], w_oth.at[:, pl.ds(0, inner)], load_sem.at[0]),
+        pltpu.make_async_copy(w_up.at[0, :, oth_cols], w_oth.at[:, pl.ds(inner, inner)], load_sem.at[1]),
+        pltpu.make_async_copy(w_gate.at[0, :, my_cols], w_mine.at[:, pl.ds(0, inner)], load_sem.at[2]),
+        pltpu.make_async_copy(w_up.at[0, :, my_cols], w_mine.at[:, pl.ds(inner, inner)], load_sem.at[3]),
+        pltpu.make_async_copy(w_down.at[0, :, my_feat], wd.at[my_rows, :], load_sem.at[4]),
+        pltpu.make_async_copy(down_scale.at[:, my_feat], ds, load_sem.at[5]),
+    ]
+    own = pltpu.make_async_copy(tokens, buf.at[me], own_sem.at[0])
+    own.start()
+
+    barrier = pltpu.get_barrier_semaphore()
+
+    def greet(i, carry):
+        pl.semaphore_signal(
+            barrier, inc=1, device_id={"local": (me + i) % experts}, device_id_type=MESH
+        )
+        return carry
+
+    lax.fori_loop(1, experts, greet, 0)
+    pl.semaphore_signal(barrier, inc=1, device_id={"node": other}, device_id_type=MESH)
+    own.wait()
+    pl.semaphore_wait(barrier, experts)
+
+    def up(b):
+        return remote(buf.at[b], buf.at[b], blk_send.at[0, b], blk_recv.at[0, b], {"local": me + 4})
+
+    def down(b):
+        return remote(buf.at[b], buf.at[b], blk_send.at[1, b], blk_recv.at[0, b], {"local": me - 4})
+
+    def to_x(b):
+        return remote(buf.at[b], buf.at[b], blk_send.at[2, b], blk_recv.at[0, b], {"local": xn})
+
+    def to_y(b):
+        return remote(buf.at[b], buf.at[b], blk_send.at[3, b], blk_recv.at[0, b], {"local": yn})
+
+    def top_x(b):
+        part = buf.at[b, pl.ds(0, half), :]
+        return remote(part, part, blk_send.at[4, b], blk_recv.at[1, b], {"local": xn})
+
+    def low_y(b):
+        part = buf.at[b, pl.ds(half, half), :]
+        return remote(part, part, blk_send.at[5, b], blk_recv.at[2, b], {"local": yn})
+
+    def column_step(s, act):
+        if s == 0:
+            act(me, z < levels - 1, z > 0)
+        else:
+            @pl.when(z >= s)
+            def _():
+                act(me - 4 * s, z < levels - 1, z < 0)
+
+            @pl.when(z + s <= levels - 1)
+            def _():
+                act(me + 4 * s, z < 0, z > 0)
+
+    def send_block(s):
+        def act(b, goes_up, goes_down):
+            if s > 0:
+                to_x(b).wait_recv()
+
+            @pl.when(goes_up)
+            def _():
+                up(b).start()
+
+            @pl.when(goes_down)
+            def _():
+                down(b).start()
+
+            to_x(b).start()
+            to_y(b).start()
+
+        column_step(s, act)
+
+    def pass_on(s):
+        def act(b, goes_up, goes_down):
+            from_y = b + yn - me
+            to_y(from_y).wait_recv()
+            top_x(from_y).start()
+            from_x = b + xn - me
+            to_x(from_x).wait_recv()
+            low_y(from_x).start()
+
+        column_step(s, act)
+
+    def sent(s):
+        def act(b, goes_up, goes_down):
+            @pl.when(goes_up)
+            def _():
+                up(b).wait_send()
+
+            @pl.when(goes_down)
+            def _():
+                down(b).wait_send()
+
+            to_x(b).wait_send()
+            to_y(b).wait_send()
+            top_x(b + yn - me).wait_send()
+            low_y(b + xn - me).wait_send()
+
+        column_step(s, act)
+
+    send_block(0)
+    for copy in loads:
+        copy.start()
+    share = remote(
+        w_down.at[0, :, oth_feat], wd.at[my_rows, :], wd_send.at[0], wd_recv.at[0], {"node": other}
+    )
+    share.start()
+
+    lane = lax.broadcasted_iota(jnp.int32, (rows, 128), 1)
+    chosen = jnp.zeros((rows, 128), F32)
+    weight = jnp.zeros((rows, 128), F32)
+    for k in range(top):
+        hit = ids[:, k:k + 1] == lane
+        chosen = chosen + jnp.where(hit, 1.0, 0.0)
+        weight = weight + jnp.where(hit, probs[:, k:k + 1], 0.0)
+    before = lax.broadcasted_iota(jnp.int32, (rows, rows), 1) < lax.broadcasted_iota(
+        jnp.int32, (rows, rows), 0
+    )
+    place = jnp.dot(
+        jnp.where(before, 1.0, 0.0).astype(BF), chosen.astype(BF), preferred_element_type=F32
+    )
+    place = jnp.where(chosen > 0.5, place, -1.0)
+    code_mat[...] = place
+    prob_mat[...] = weight
+    place_t = place.T
+    for e in range(experts):
+        codes_out[e] = jnp.broadcast_to(place_t[e:e + 1, :], (8, rows))
+    codes_in[me] = codes_out[me]
+
+    def code(to):
+        return remote(
+            codes_out.at[to], codes_in.at[me], code_send.at[to], code_recv.at[me], {"local": to}
+        )
+
+    def code_from(e):
+        return remote(
+            codes_out.at[e], codes_in.at[e], code_send.at[e], code_recv.at[e], {"local": e}
+        )
+
+    def send_code(i, carry):
+        code((me + i) % experts).start()
+        return carry
+
+    lax.fori_loop(1, experts, send_code, 0)
+
+    for s in range(1, levels):
+        send_block(s)
+        pass_on(s - 1)
+    for copy in loads:
+        copy.wait()
+
+    def give(to):
+        return remote(
+            outb.at[to], ret.at[me], ret_send.at[to], ret_recv.at[me], {"local": to}
+        )
+
+    def give_from(e):
+        return remote(outb.at[e], ret.at[e], ret_send.at[e], ret_recv.at[e], {"local": e})
+
+    def column_of(g):
+        gx, gy = g // 2, g % 2
+        return (y + gy * (1 - 2 * y)) * 2 + x + gx * (1 - 2 * x)
+
+    slot_row = lax.broadcasted_iota(jnp.int32, (cap, rows), 0).astype(F32)
+
+    def run(g):
+        col = column_of(g)
+
+        def fill(i, carry):
+            b = i * 4 + col
+
+            @pl.when(b != me)
+            def _():
+                code_from(b).wait_recv()
+
+            pick = jnp.where(codes_in[b][0:1, :] == slot_row, 1.0, 0.0).astype(BF)
+            slots[pl.ds(pl.multiple_of(i * cap, 16), cap), :] = jnp.dot(
+                pick, buf[b], preferred_element_type=F32
+            ).astype(BF)
+            return carry
+
+        lax.fori_loop(0, levels, fill, 0)
+
+        def for_other(j, carry):
+            cols = pl.ds(pl.multiple_of(j * 256, 256), 256)
+            psend[g, :, cols] = jnp.dot(
+                slots[...], w_oth[:, cols], preferred_element_type=F32
+            ).astype(BF)
+            return carry
+
+        lax.fori_loop(0, 2 * inner // 256, for_other, 0)
+        part = remote(
+            psend.at[g], precv.at[g], part_send.at[g], part_recv.at[g], {"node": other}
+        )
+        part.start()
+
+        def for_me(j, carry):
+            cols = pl.ds(pl.multiple_of(j * 256, 256), 256)
+            mine[:, cols] = jnp.dot(slots[...], w_mine[:, cols], preferred_element_type=F32)
+            return carry
+
+        lax.fori_loop(0, 2 * inner // 256, for_me, 0)
+        part.wait()
+
+        def act(i, carry):
+            r = pl.ds(pl.multiple_of(i * cap, 16), cap)
+            gate = mine[r, 0:inner] + precv[g, r, 0:inner].astype(F32)
+            upv = mine[r, inner:2 * inner] + precv[g, r, inner:2 * inner].astype(F32)
+            gate = gate * gate_scale[...]
+            hid[g, nd, r, :] = (gate / (1.0 + jnp.exp(-gate)) * (upv * up_scale[...])).astype(BF)
+            return carry
+
+        lax.fori_loop(0, levels, act, 0)
+        swap = remote(
+            hid.at[g, nd], hid.at[g, nd], hid_send.at[g], hid_recv.at[g], {"node": other}
+        )
+        swap.start()
+        swap.wait()
+
+        def project(j, carry):
+            cols = pl.ds(pl.multiple_of(j * 256, 256), 256)
+            value = jnp.dot(hid[g, 0], wd[0:inner, cols], preferred_element_type=F32)
+            value = value + jnp.dot(
+                hid[g, 1], wd[inner:2 * inner, cols], preferred_element_type=F32
+            )
+            value = (value * ds[:, cols]).astype(BF)
+            for i in range(levels):
+                outb[i * 4 + col, :, cols] = value[i * cap:(i + 1) * cap]
+            return carry
+
+        lax.fori_loop(0, width // 256, project, 0)
+
+        def back(i, carry):
+            b = i * 4 + col
+
+            @pl.when(b != me)
+            def _():
+                give(b).start()
+
+            return carry
+
+        lax.fori_loop(0, levels, back, 0)
+
+    share.wait()
+    run(0)
+    keep = pltpu.make_async_copy(outb.at[me], ret.at[me], own_sem.at[1])
+    keep.start()
+    pass_on(levels - 1)
+
+    def later(g, carry):
+        @pl.when(g == 3)
+        def _():
+            def diag(i, inner_carry):
+                b = i * 4 + 3 - c
+                top_x(b).wait_recv()
+                low_y(b).wait_recv()
+                return inner_carry
+
+            lax.fori_loop(0, levels, diag, 0)
+
+        run(g)
+        return carry
+
+    lax.fori_loop(1, 4, later, 0)
+    keep.wait()
+
+    acc[...] = jnp.zeros_like(acc)
+    dots[...] = jnp.zeros_like(dots)
+    slot_lane = lax.broadcasted_iota(jnp.int32, (rows, cap), 1).astype(F32)
+
+    def combine(i, carry):
+        e = (i % levels) * 4 + column_of(i // levels)
+
+        @pl.when(e != me)
+        def _():
+            give_from(e).wait_recv()
+
+        at_e = lane == e
+        slot = jnp.sum(jnp.where(at_e, code_mat[...], 0.0), axis=1, keepdims=True)
+        prob = jnp.sum(jnp.where(at_e, prob_mat[...], 0.0), axis=1, keepdims=True)
+        pick = jnp.where(slot == slot_lane, 1.0, 0.0).astype(BF)
+        total = jnp.zeros((rows, 1), F32)
+        for j in range(width // 256):
+            cols = slice(j * 256, (j + 1) * 256)
+            got = jnp.dot(pick, ret[e, :, cols], preferred_element_type=F32)
+            acc[:, cols] += got * prob
+            total = total + jnp.sum(got * cot[:, cols].astype(F32), axis=1, keepdims=True)
+        dots[...] = jnp.where(at_e, total, dots[...])
+        return carry
+
+    lax.fori_loop(0, experts, combine, 0)
+    join = remote(dots, dots_in, dot_send.at[0], dot_recv.at[0], {"node": other})
+    join.start()
+    mixed[...] = acc[...].astype(BF)
+    join.wait()
+    both = dots[...] + dots_in[...]
+    small = lax.broadcasted_iota(jnp.int32, (rows, top), 1)
+    grads = jnp.zeros((rows, top), F32)
+    for k in range(top):
+        one = jnp.sum(jnp.where(ids[:, k:k + 1] == lane, both, 0.0), axis=1, keepdims=True)
+        grads = jnp.where(small == k, one, grads)
+    gate_grad[...] = grads
+
+    for s in range(levels):
+        sent(s)
+
+    def finish(i, carry):
+        to = (me + i) % experts
+        code(to).wait_send()
+        give(to).wait_send()
+        return carry
+
+    lax.fori_loop(1, experts, finish, 0)
+
+
+def fused(
+    tokens, expert_ids, gate_probs, w_gate, w_up, w_down, gate_scale, up_scale, down_scale, cotangent
+):
+    experts = lax.axis_size("local")
+    rows, top = expert_ids.shape
+    cap = max(2, min(rows, rows * top * 5 // (4 * experts)))
+    width = tokens.shape[1]
+    inner = w_down.shape[1]
+    levels = experts // 4
+    m = levels * cap
+    vm = pl.BlockSpec(memory_space=pltpu.VMEM)
+    hbm = pl.BlockSpec(memory_space=pl.ANY)
+    dma = pltpu.SemaphoreType.DMA
+    return pl.pallas_call(
+        layer_kernel,
+        out_shape=(
+            jax.ShapeDtypeStruct((rows, width), BF),
+            jax.ShapeDtypeStruct((rows, top), F32),
+        ),
+        in_specs=[hbm, vm, vm, hbm, hbm, hbm, vm, vm, hbm, vm],
+        out_specs=(vm, vm),
+        scratch_shapes=[
+            pltpu.VMEM((experts, rows, width), BF),
+            pltpu.VMEM((width, 2 * inner), BF),
+            pltpu.VMEM((width, 2 * inner), BF),
+            pltpu.VMEM((2 * inner, width), BF),
+            pltpu.VMEM((1, width), F32),
+            pltpu.VMEM((experts, 8, rows), F32),
+            pltpu.VMEM((experts, 8, rows), F32),
+            pltpu.VMEM((rows, 128), F32),
+            pltpu.VMEM((rows, 128), F32),
+            pltpu.VMEM((m, width), BF),
+            pltpu.VMEM((4, m, 2 * inner), BF),
+            pltpu.VMEM((4, m, 2 * inner), BF),
+            pltpu.VMEM((m, 2 * inner), F32),
+            pltpu.VMEM((4, 2, m, inner), BF),
+            pltpu.VMEM((experts, cap, width), BF),
+            pltpu.VMEM((experts, cap, width), BF),
+            pltpu.VMEM((rows, width), F32),
+            pltpu.VMEM((rows, 128), F32),
+            pltpu.VMEM((rows, 128), F32),
+            dma((6,)),
+            dma((2,)),
+            dma((6, experts)),
+            dma((3, experts)),
+            dma((experts,)),
+            dma((experts,)),
+            dma((4,)),
+            dma((4,)),
+            dma((4,)),
+            dma((4,)),
+            dma((experts,)),
+            dma((experts,)),
+            dma((1,)),
+            dma((1,)),
+            dma((1,)),
+            dma((1,)),
+        ],
+        compiler_params=pltpu.CompilerParams(
+            collective_id=0, has_side_effects=True, vmem_limit_bytes=56 * 1024 * 1024
+        ),
+    )(
+        tokens, expert_ids, gate_probs, w_gate, w_up, w_down, gate_scale, up_scale, down_scale,
+        cotangent,
+    )
+
+
 def solution(mesh):
+    small = mesh.shape["local"] == 16 and mesh.shape["node"] == 2
     return jax.shard_map(
-        on_device,
+        fused if small else on_device,
         mesh=mesh,
         in_specs=(
             P(("groups", "local"), "node"),

time: 346 us -> 178 us (0.51)
  the two profiles are of different devices: /device:TPU:15 before, /device:TPU:27 now
where the time goes in v1:
time: 178 us; the launch traced here: 177 us
  Pallas kernels  171 us (96%)
  local copies, waits for them, and re-layouts  6.14 us (3%)
    pallas_call x1, Pallas kernels, fused(): pl.pallas_call(layer_kernel, out_shape=(jax.ShapeDtypeStruct((rows, width...  171 us
    unnamed x3, local copies, waits for them, and re-layouts  4.64 us

profile of v1, /device:TPU:27, one launch (start us, length us, event | category | flops | bytes accessed | tf_op | source)
XLA Modules:
  0.0 177.4 jit_solution(9134424360785518382)
XLA Ops:
  0.6 1.4 copy.12.ids
  2.0 1.4 copy.13.probs
  3.5 170.7 %shard_map.113 = (bf16[128,1792]{1,0:T(8,128)(2,1)}, f32[128,8]{1,0:T(8,128)}) custom-call(bf16[128,1792]{1,0:T(8,128)(2,1)} %tokens.1, s32[128,8]{1,0:T(8,128)} %copy.12.ids, f32[128,8]{1,0:T(8,128)} %copy.13.probs, bf16[1,1792,1024]{2,1,0:T(8,128)(2,1)} %w_gate.1, bf16[1,1792,1024]{2,1,0:T(8,128)(2,1)} %w_up.1, bf16[1,512,3584]{2,1,0:T(8,128)(2,1)} %w_down.1, ...), custom_call_target="tpu_custom_call" | custom-call | tf_op jit(solution)/shard_map/pallas_call | solution.py:434
  174.1 1.5 copy.14
  175.6 1.8 %copy.16 = bf16[128,1792]{1,0:T(8,128)(2,1)} copy(bf16[128,1792]{1,0:T(8,128)(2,1)} %get-tuple-element.6) | data formatting | bytes 917504

commit v2 on v0

--- a/solution.py
+++ b/solution.py
@@ -2,6 +2,13 @@
 import jax.numpy as jnp
 from jax import lax
 from jax.sharding import PartitionSpec as P
+from jax.experimental import pallas as pl
+from jax.experimental.pallas import tpu as pltpu
+
+
+MESH = pl.DeviceIdType.MESH
+BF = jnp.bfloat16
+F32 = jnp.float32
 
 
 def on_device(
@@ -61,9 +68,432 @@
     return (combined, gate_grad)
 
 
+def layer_kernel(
+    tokens, ids, probs, w_gate, w_up, w_down, gate_scale, up_scale, down_scale, cot,
+    mixed, gate_grad,
+    blk, cotb, info, w_mine, w_oth, wd, ds, picked, slots, psend, precv, mine, hid,
+    outb, ret, acc, part_out, part_in, dots_out, dots_in, dots, dots_core,
+    load_sem, own_sem, keep_sem, line_send, line_recv, disp_send, disp_recv,
+    gu_send, gu_recv, hid_send, hid_recv, ret_send, ret_recv, back_send, back_recv,
+    core_send, core_recv,
+):
+    levels, rows, width = blk.shape
+    plane, cap = ret.shape[1], ret.shape[2]
+    inner = gate_scale.shape[1]
+    top = ids.shape[1]
+    experts = levels * plane
+    me = lax.axis_index("local")
+    nd = lax.axis_index("node")
+    z, c = me // 4, me % 4
+    y, x = c // 2, c % 2
+    other = 1 - nd
+
+    def remote(src, dst, send, recv, where):
+        return pltpu.make_async_remote_copy(
+            src_ref=src, dst_ref=dst, send_sem=send, recv_sem=recv,
+            device_id=where, device_id_type=MESH,
+        )
+
+    order = [z, 1 + z % 2, 3 - 3 * (z // 2), 2 - 2 * (z % 2) + z // 2]
+
+    def column(j):
+        return (y + (j // 2) * (1 - 2 * y)) * 2 + x + (j % 2) * (1 - 2 * x)
+
+    my_cols = pl.ds(pl.multiple_of(nd * inner, 128), inner)
+    oth_cols = pl.ds(pl.multiple_of(other * inner, 128), inner)
+    my_feat = pl.ds(pl.multiple_of(nd * width, 128), width)
+    oth_feat = pl.ds(pl.multiple_of(other * width, 128), width)
+    my_rows = pl.ds(pl.multiple_of(nd * inner, 128), inner)
+    loads = [
+        pltpu.make_async_copy(w_gate.at[0, :, oth_cols], w_oth.at[:, pl.ds(0, inner)], load_sem.at[0]),
+        pltpu.make_async_copy(w_up.at[0, :, oth_cols], w_oth.at[:, pl.ds(inner, inner)], load_sem.at[1]),
+        pltpu.make_async_copy(w_gate.at[0, :, my_cols], w_mine.at[:, pl.ds(0, inner)], load_sem.at[2]),
+        pltpu.make_async_copy(w_up.at[0, :, my_cols], w_mine.at[:, pl.ds(inner, inner)], load_sem.at[3]),
+        pltpu.make_async_copy(w_down.at[0, :, my_feat], wd.at[my_rows, :], load_sem.at[4]),
+        pltpu.make_async_copy(down_scale.at[:, my_feat], ds, load_sem.at[5]),
+    ]
+    own = [
+        pltpu.make_async_copy(tokens, blk.at[z], own_sem.at[0]),
+        pltpu.make_async_copy(cot, cotb.at[z], own_sem.at[1]),
+    ]
+    for copy in own:
+        copy.start()
+
+    barrier = pltpu.get_barrier_semaphore()
+    for i in range(1, levels):
+        pl.semaphore_signal(
+            barrier, inc=1, device_id={"local": (me + plane * i) % experts}, device_id_type=MESH
+        )
+    for j in range(1, plane):
+        pl.semaphore_signal(
+            barrier, inc=1, device_id={"local": z * plane + column(j)}, device_id_type=MESH
+        )
+    pl.semaphore_signal(barrier, inc=1, device_id={"node": other}, device_id_type=MESH)
+
+    lane = lax.broadcasted_iota(jnp.int32, (rows, 128), 1)
+    chosen = jnp.zeros((rows, 128), F32)
+    weight = jnp.zeros((rows, 128), F32)
+    for k in range(top):
+        hit = ids[:, k:k + 1] == lane
+        chosen = chosen + jnp.where(hit, 1.0, 0.0)
+        weight = weight + jnp.where(hit, probs[:, k:k + 1], 0.0)
+    before = lax.broadcasted_iota(jnp.int32, (rows, rows), 1) < lax.broadcasted_iota(
+        jnp.int32, (rows, rows), 0
+    )
+    place = jnp.dot(
+        jnp.where(before, 1.0, 0.0).astype(BF), chosen.astype(BF), preferred_element_type=F32
+    )
+    place = jnp.where(chosen > 0.5, place, -1.0)
+    info[z, 0:rows, :] = place
+    info[z, rows:2 * rows, :] = weight
+    info[z, 2 * rows:2 * rows + experts, :] = place.T[0:experts, :]
+    for copy in own:
+        copy.wait()
+    pl.semaphore_wait(barrier, levels + plane - 1)
+
+    items = (info, blk, cotb)
+
+    def line(item, up, b):
+        return remote(
+            items[item].at[b], items[item].at[b],
+            line_send.at[1 - up, item, b], line_recv.at[item, b],
+            {"local": me - plane + 2 * plane * up},
+        )
+
+    def line_step(s, act):
+        if s == 0:
+            act(z, z < levels - 1, z > 0)
+        else:
+            @pl.when(z >= s)
+            def _():
+                act(z - s, z < levels - 1, z < 0)
+
+            @pl.when(z + s <= levels - 1)
+            def _():
+                act(z + s, z < 0, z > 0)
+
+    def spread(s, which):
+        def act(b, goes_up, goes_down):
+            for item in which:
+                if s > 0:
+                    line(item, 1, b).wait_recv()
+
+                @pl.when(goes_up)
+                def _():
+                    line(item, 1, b).start()
+
+                @pl.when(goes_down)
+                def _():
+                    line(item, 0, b).start()
+
+        line_step(s, act)
+
+    def spread_done(s):
+        def act(b, goes_up, goes_down):
+            for item in range(3):
+                @pl.when(goes_up)
+                def _():
+                    line(item, 1, b).wait_send()
+
+                @pl.when(goes_down)
+                def _():
+                    line(item, 0, b).wait_send()
+
+        line_step(s, act)
+
+    slot_row = lax.broadcasted_iota(jnp.int32, (cap, rows), 0).astype(F32)
+
+    def slots_of(i):
+        return pl.ds(pl.multiple_of(i * cap, 16), cap)
+
+    def disp(b, to):
+        return remote(
+            picked.at[b, to], slots.at[b, slots_of(c), :],
+            disp_send.at[b, to], disp_recv.at[b, c], {"local": z * plane + to},
+        )
+
+    def disp_from(b, i):
+        return remote(
+            picked.at[b, i], slots.at[b, slots_of(i), :],
+            disp_send.at[b, i], disp_recv.at[b, i], {"local": z * plane + i},
+        )
+
+    def dispatch(b):
+        for j in (3, 1, 2, 0):
+            to = column(j)
+            code = info[b, pl.ds(2 * rows + z * plane + to, 1), :]
+            pick = jnp.where(code == slot_row, 1.0, 0.0).astype(BF)
+            for n in range(width // 256):
+                cols = slice(n * 256, (n + 1) * 256)
+                value = jnp.dot(pick, blk[b, :, cols], preferred_element_type=F32).astype(BF)
+                if j == 0:
+                    slots[b, slots_of(c), cols] = value
+                else:
+                    picked[b, to, :, cols] = value
+            if j > 0:
+                disp(b, to).start()
+
+    def give(b, to):
+        return remote(
+            outb.at[b, slots_of(to), :], ret.at[b, c],
+            ret_send.at[b, to], ret_recv.at[b, c], {"local": z * plane + to},
+        )
+
+    def give_from(b, i):
+        return remote(
+            outb.at[b, slots_of(i), :], ret.at[b, i],
+            ret_send.at[b, i], ret_recv.at[b, i], {"local": z * plane + i},
+        )
+
+    def keep(b):
+        return pltpu.make_async_copy(outb.at[b, slots_of(c), :], ret.at[b, c], keep_sem.at[b])
+
+    def run(b):
+        for j in range(1, plane):
+            disp_from(b, column(j)).wait_recv()
+
+        def for_other(n, carry):
+            cols = pl.ds(pl.multiple_of(n * 256, 256), 256)
+            psend[b, :, cols] = jnp.dot(
+                slots[b], w_oth[:, cols], preferred_element_type=F32
+            ).astype(BF)
+            return carry
+
+        lax.fori_loop(0, 2 * inner // 256, for_other, 0)
+        part = remote(psend.at[b], precv.at[b], gu_send.at[b], gu_recv.at[b], {"node": other})
+        part.start()
+
+        def for_me(n, carry):
+            cols = pl.ds(pl.multiple_of(n * 256, 256), 256)
+            mine[:, cols] = jnp.dot(slots[b], w_mine[:, cols], preferred_element_type=F32)
+            return carry
+
+        lax.fori_loop(0, 2 * inner // 256, for_me, 0)
+        part.wait()
+
+        def act(i, carry):
+            r = slots_of(i)
+            gate = mine[r, 0:inner] + precv[b, r, 0:inner].astype(F32)
+            upv = mine[r, inner:2 * inner] + precv[b, r, inner:2 * inner].astype(F32)
+            gate = gate * gate_scale[...]
+            hid[b, nd, r, :] = (gate / (1.0 + jnp.exp(-gate)) * (upv * up_scale[...])).astype(BF)
+            return carry
+
+        lax.fori_loop(0, plane, act, 0)
+        swap = remote(
+            hid.at[b, nd], hid.at[b, nd], hid_send.at[b], hid_recv.at[b], {"node": other}
+        )
+        swap.start()
+        swap.wait()
+
+        def project(n, carry):
+            cols = pl.ds(pl.multiple_of(n * 256, 256), 256)
+            value = jnp.dot(hid[b, 0], wd[0:inner, cols], preferred_element_type=F32)
+            value = value + jnp.dot(
+                hid[b, 1], wd[inner:2 * inner, cols], preferred_element_type=F32
+            )
+            outb[b, :, cols] = (value * ds[:, cols]).astype(BF)
+            return carry
+
+        lax.fori_loop(0, width // 256, project, 0)
+        for j in (3, 1, 2):
+            give(b, column(j)).start()
+        keep(b).start()
+
+    slot_lane = lax.broadcasted_iota(jnp.int32, (rows, cap), 1).astype(F32)
+
+    def home(b):
+        to = {"local": b * plane + c}
+        return (
+            remote(part_out.at[b], part_in.at[z], back_send.at[0, b], back_recv.at[0, z], to),
+            remote(dots_out.at[b], dots_in.at[z], back_send.at[1, b], back_recv.at[1, z], to),
+        )
+
+    def home_from(b):
+        to = {"local": b * plane + c}
+        return (
+            remote(part_out.at[b], part_in.at[b], back_send.at[0, b], back_recv.at[0, b], to),
+            remote(dots_out.at[b], dots_in.at[b], back_send.at[1, b], back_recv.at[1, b], to),
+        )
+
+    def combine(b, stays):
+        acc[...] = jnp.zeros_like(acc)
+        dots[...] = jnp.zeros_like(dots)
+
+        def one(j, carry):
+            i = column(j)
+
+            @pl.when(j > 0)
+            def _():
+                give_from(b, i).wait_recv()
+
+            at_e = lane == z * plane + i
+            slot = jnp.sum(jnp.where(at_e, info[b, 0:rows, :], 0.0), axis=1, keepdims=True)
+            prob = jnp.sum(
+                jnp.where(at_e, info[b, rows:2 * rows, :], 0.0), axis=1, keepdims=True
+            )
+            pick = jnp.where(slot == slot_lane, 1.0, 0.0).astype(BF)
+            total = jnp.zeros((rows, 1), F32)
+            for n in range(width // 256):
+                cols = slice(n * 256, (n + 1) * 256)
+                got = jnp.dot(pick, ret[b, i, :, cols], preferred_element_type=F32)
+                acc[:, cols] += got * prob
+                total = total + jnp.sum(
+                    got * cotb[b, :, cols].astype(F32), axis=1, keepdims=True
+                )
+            dots[...] = jnp.where(at_e, total, dots[...])
+            return carry
+
+        keep(b).wait()
+        lax.fori_loop(0, plane, one, 0)
+        if stays:
+            part_in[b] = acc[...].astype(BF)
+            dots_in[b] = dots[...]
+        else:
+            part_out[b] = acc[...].astype(BF)
+            dots_out[b] = dots[...]
+            for copy in home(b):
+                copy.start()
+
+    spread(0, (0, 1))
+    for copy in loads:
+        copy.start()
+    share = remote(
+        w_down.at[0, :, oth_feat], wd.at[my_rows, :], core_send.at[0], core_recv.at[0],
+        {"node": other},
+    )
+    share.start()
+    dispatch(order[0])
+    spread(1, (0, 1))
+    dispatch(order[1])
+    spread(2, (0, 1))
+    for copy in loads:
+        copy.wait()
+    share.wait()
+    run(order[0])
+    spread(3, (0, 1))
+    spread(0, (2,))
+    dispatch(order[2])
+    dispatch(order[3])
+    run(order[1])
+    spread(1, (2,))
+    combine(order[0], True)
+    spread(2, (2,))
+    run(order[2])
+    spread(3, (2,))
+    combine(order[1], False)
+    run(order[3])
+    combine(order[2], False)
+    combine(order[3], False)
+
+    for s in range(1, levels):
+        for copy in home_from((z + s) % levels):
+            copy.wait_recv()
+    dots[...] = dots_in[0] + dots_in[1] + dots_in[2] + dots_in[3]
+    join = remote(dots, dots_core, core_send.at[1], core_recv.at[1], {"node": other})
+    join.start()
+    for n in range(width // 256):
+        cols = slice(n * 256, (n + 1) * 256)
+        total = part_in[0, :, cols].astype(F32)
+        for i in range(1, levels):
+            total = total + part_in[i, :, cols].astype(F32)
+        mixed[:, cols] = total.astype(BF)
+    join.wait()
+    both = dots[...] + dots_core[...]
+    small = lax.broadcasted_iota(jnp.int32, (rows, top), 1)
+    grads = jnp.zeros((rows, top), F32)
+    for k in range(top):
+        one = jnp.sum(jnp.where(ids[:, k:k + 1] == lane, both, 0.0), axis=1, keepdims=True)
+        grads = jnp.where(small == k, one, grads)
+    gate_grad[...] = grads
+
+    for s in range(levels):
+        spread_done(s)
+    for i in range(levels):
+        for j in range(1, plane):
+            disp(i, column(j)).wait_send()
+            give(i, column(j)).wait_send()
+    for s in range(1, levels):
+        for copy in home((z + s) % levels):
+            copy.wait_send()
+
+
+def fused(
+    tokens, expert_ids, gate_probs, w_gate, w_up, w_down, gate_scale, up_scale, down_scale, cotangent
+):
+    experts = lax.axis_size("local")
+    rows, top = expert_ids.shape
+    cap = max(2, min(rows, rows * top * 5 // (4 * experts)))
+    width = tokens.shape[1]
+    inner = w_down.shape[1]
+    plane = 4
+    levels = experts // plane
+    m = plane * cap
+    vm = pl.BlockSpec(memory_space=pltpu.VMEM)
+    hbm = pl.BlockSpec(memory_space=pl.ANY)
+    dma = pltpu.SemaphoreType.DMA
+    return pl.pallas_call(
+        layer_kernel,
+        out_shape=(
+            jax.ShapeDtypeStruct((rows, width), BF),
+            jax.ShapeDtypeStruct((rows, top), F32),
+        ),
+        in_specs=[hbm, vm, vm, hbm, hbm, hbm, vm, vm, hbm, hbm],
+        out_specs=(vm, vm),
+        scratch_shapes=[
+            pltpu.VMEM((levels, rows, width), BF),
+            pltpu.VMEM((levels, rows, width), BF),
+            pltpu.VMEM((levels, 2 * rows + experts, 128), F32),
+            pltpu.VMEM((width, 2 * inner), BF),
+            pltpu.VMEM((width, 2 * inner), BF),
+            pltpu.VMEM((2 * inner, width), BF),
+            pltpu.VMEM((1, width), F32),
+            pltpu.VMEM((levels, plane, cap, width), BF),
+            pltpu.VMEM((levels, m, width), BF),
+            pltpu.VMEM((levels, m, 2 * inner), BF),
+            pltpu.VMEM((levels, m, 2 * inner), BF),
+            pltpu.VMEM((m, 2 * inner), F32),
+            pltpu.VMEM((levels, 2, m, inner), BF),
+            pltpu.VMEM((levels, m, width), BF),
+            pltpu.VMEM((levels, plane, cap, width), BF),
+            pltpu.VMEM((rows, width), F32),
+            pltpu.VMEM((levels, rows, width), BF),
+            pltpu.VMEM((levels, rows, width), BF),
+            pltpu.VMEM((levels, rows, 128), F32),
+            pltpu.VMEM((levels, rows, 128), F32),
+            pltpu.VMEM((rows, 128), F32),
+            pltpu.VMEM((rows, 128), F32),
+            dma((6,)),
+            dma((2,)),
+            dma((levels,)),
+            dma((2, 3, levels)),
+            dma((3, levels)),
+            dma((levels, plane)),
+            dma((levels, plane)),
+            dma((levels,)),
+            dma((levels,)),
+            dma((levels,)),
+            dma((levels,)),
+            dma((levels, plane)),
+            dma((levels, plane)),
+            dma((2, levels)),
+            dma((2, levels)),
+            dma((2,)),
+            dma((2,)),
+        ],
+        compiler_params=pltpu.CompilerParams(
+            collective_id=0, has_side_effects=True, vmem_limit_bytes=58 * 1024 * 1024
+        ),
+    )(
+        tokens, expert_ids, gate_probs, w_gate, w_up, w_down, gate_scale, up_scale, down_scale,
+        cotangent,
+    )
+
+
 def solution(mesh):
+    small = mesh.shape["local"] == 16 and mesh.shape["node"] == 2
     return jax.shard_map(
-        on_device,
+        fused if small else on_device,
         mesh=mesh,
         in_specs=(
             P(("groups", "local"), "node"),

time: 346 us -> 153 us (0.44)
  the two profiles are of different devices: /device:TPU:15 before, /device:TPU:27 now
where the time goes in v2:
time: 153 us; the launch traced here: 151 us
  Pallas kernels  144 us (94%)
  local copies, waits for them, and re-layouts  6.14 us (4%)
    pallas_call x1, Pallas kernels, fused(): pl.pallas_call(layer_kernel, out_shape=(jax.ShapeDtypeStruct((rows, width...  144 us
    unnamed x3, local copies, waits for them, and re-layouts  4.64 us

profile of v2, /device:TPU:27, one launch (start us, length us, event | category | flops | bytes accessed | tf_op | source)
XLA Modules:
  0.0 150.6 jit_solution(15776515710093442811)
XLA Ops:
  0.6 1.4 copy.12.ids
  2.0 1.4 copy.13.probs
  3.5 143.8 %shard_map.113 = (bf16[128,1792]{1,0:T(8,128)(2,1)}, f32[128,8]{1,0:T(8,128)}) custom-call(bf16[128,1792]{1,0:T(8,128)(2,1)} %tokens.1, s32[128,8]{1,0:T(8,128)} %copy.12.ids, f32[128,8]{1,0:T(8,128)} %copy.13.probs, bf16[1,1792,1024]{2,1,0:T(8,128)(2,1)} %w_gate.1, bf16[1,1792,1024]{2,1,0:T(8,128)(2,1)} %w_up.1, bf16[1,512,3584]{2,1,0:T(8,128)(2,1)} %w_down.1, ...), custom_call_target="tpu_custom_call" | custom-call | tf_op jit(solution)/shard_map/pallas_call | solution.py:435
  147.3 1.5 copy.14
  148.8 1.8 %copy.16 = bf16[128,1792]{1,0:T(8,128)(2,1)} copy(bf16[128,1792]{1,0:T(8,128)(2,1)} %get-tuple-element.6) | data formatting | bytes 917504

commit v3 on v2

--- a/solution.py
+++ b/solution.py
@@ -72,7 +72,7 @@
     tokens, ids, probs, w_gate, w_up, w_down, gate_scale, up_scale, down_scale, cot,
     mixed, gate_grad,
     blk, cotb, info, w_mine, w_oth, wd, ds, picked, slots, psend, precv, mine, hid,
-    outb, ret, acc, part_out, part_in, dots_out, dots_in, dots, dots_core,
+    outb, ret, acc, part_out, part_in, dots_out, dots_in, table, dots, dots_sum, dots_core,
     load_sem, own_sem, keep_sem, line_send, line_recv, disp_send, disp_recv,
     gu_send, gu_recv, hid_send, hid_recv, ret_send, ret_recv, back_send, back_recv,
     core_send, core_recv,
@@ -80,7 +80,7 @@
     levels, rows, width = blk.shape
     plane, cap = ret.shape[1], ret.shape[2]
     inner = gate_scale.shape[1]
-    top = ids.shape[1]
+    top = ids.shape[0]
     experts = levels * plane
     me = lax.axis_index("local")
     nd = lax.axis_index("node")
@@ -130,23 +130,21 @@
         )
     pl.semaphore_signal(barrier, inc=1, device_id={"node": other}, device_id_type=MESH)
 
-    lane = lax.broadcasted_iota(jnp.int32, (rows, 128), 1)
-    chosen = jnp.zeros((rows, 128), F32)
-    weight = jnp.zeros((rows, 128), F32)
+    expert_row = lax.broadcasted_iota(jnp.int32, (experts, rows), 0)
+    chosen = jnp.zeros((experts, rows), F32)
+    weight = jnp.zeros((experts, rows), F32)
     for k in range(top):
-        hit = ids[:, k:k + 1] == lane
+        hit = ids[k:k + 1, :] == expert_row
         chosen = chosen + jnp.where(hit, 1.0, 0.0)
-        weight = weight + jnp.where(hit, probs[:, k:k + 1], 0.0)
-    before = lax.broadcasted_iota(jnp.int32, (rows, rows), 1) < lax.broadcasted_iota(
-        jnp.int32, (rows, rows), 0
+        weight = weight + jnp.where(hit, probs[k:k + 1, :], 0.0)
+    before = lax.broadcasted_iota(jnp.int32, (rows, rows), 0) < lax.broadcasted_iota(
+        jnp.int32, (rows, rows), 1
     )
     place = jnp.dot(
-        jnp.where(before, 1.0, 0.0).astype(BF), chosen.astype(BF), preferred_element_type=F32
-    )
-    place = jnp.where(chosen > 0.5, place, -1.0)
-    info[z, 0:rows, :] = place
-    info[z, rows:2 * rows, :] = weight
-    info[z, 2 * rows:2 * rows + experts, :] = place.T[0:experts, :]
+        chosen.astype(BF), jnp.where(before, 1.0, 0.0).astype(BF), preferred_element_type=F32
+    )
+    info[z, 0:experts, :] = jnp.where(chosen > 0.5, place, -1.0)
+    info[z, experts:2 * experts, :] = weight
     for copy in own:
         copy.wait()
     pl.semaphore_wait(barrier, levels + plane - 1)
@@ -221,7 +219,7 @@
     def dispatch(b):
         for j in (3, 1, 2, 0):
             to = column(j)
-            code = info[b, pl.ds(2 * rows + z * plane + to, 1), :]
+            code = info[b, pl.ds(z * plane + to, 1), :]
             pick = jnp.where(code == slot_row, 1.0, 0.0).astype(BF)
             for n in range(width // 256):
                 cols = slice(n * 256, (n + 1) * 256)
@@ -300,6 +298,7 @@
             give(b, column(j)).start()
         keep(b).start()
 
+    lane = lax.broadcasted_iota(jnp.int32, (rows, 128), 1)
     slot_lane = lax.broadcasted_iota(jnp.int32, (rows, cap), 1).astype(F32)
 
     def home(b):
@@ -319,6 +318,9 @@
     def combine(b, stays):
         acc[...] = jnp.zeros_like(acc)
         dots[...] = jnp.zeros_like(dots)
+        table[...] = jnp.concatenate(
+            [info[b], jnp.zeros((128 - 2 * experts, rows), F32)], axis=0
+        ).T
 
         def one(j, carry):
             i = column(j)
@@ -328,10 +330,9 @@
                 give_from(b, i).wait_recv()
 
             at_e = lane == z * plane + i
-            slot = jnp.sum(jnp.where(at_e, info[b, 0:rows, :], 0.0), axis=1, keepdims=True)
-            prob = jnp.sum(
-                jnp.where(at_e, info[b, rows:2 * rows, :], 0.0), axis=1, keepdims=True
-            )
+            slot = jnp.sum(jnp.where(at_e, table[...], 0.0), axis=1, keepdims=True)
+            at_p = lane == experts + z * plane + i
+            prob = jnp.sum(jnp.where(at_p, table[...], 0.0), axis=1, keepdims=True)
             pick = jnp.where(slot == slot_lane, 1.0, 0.0).astype(BF)
             total = jnp.zeros((rows, 1), F32)
             for n in range(width // 256):
@@ -348,10 +349,10 @@
         lax.fori_loop(0, plane, one, 0)
         if stays:
             part_in[b] = acc[...].astype(BF)
-            dots_in[b] = dots[...]
+            dots_in[b] = dots[...].T[0:experts, :]
         else:
             part_out[b] = acc[...].astype(BF)
-            dots_out[b] = dots[...]
+            dots_out[b] = dots[...].T[0:experts, :]
             for copy in home(b):
                 copy.start()
 
@@ -367,30 +368,30 @@
     spread(1, (0, 1))
     dispatch(order[1])
     spread(2, (0, 1))
+    dispatch(order[3])
     for copy in loads:
         copy.wait()
     share.wait()
-    run(order[0])
     spread(3, (0, 1))
+    dispatch(order[2])
     spread(0, (2,))
-    dispatch(order[2])
-    dispatch(order[3])
     run(order[1])
     spread(1, (2,))
-    combine(order[0], True)
+    run(order[3])
     spread(2, (2,))
     run(order[2])
     spread(3, (2,))
     combine(order[1], False)
-    run(order[3])
+    run(order[0])
+    combine(order[3], False)
     combine(order[2], False)
-    combine(order[3], False)
+    combine(order[0], True)
 
     for s in range(1, levels):
         for copy in home_from((z + s) % levels):
             copy.wait_recv()
-    dots[...] = dots_in[0] + dots_in[1] + dots_in[2] + dots_in[3]
-    join = remote(dots, dots_core, core_send.at[1], core_recv.at[1], {"node": other})
+    dots_sum[...] = dots_in[0] + dots_in[1] + dots_in[2] + dots_in[3]
+    join = remote(dots_sum, dots_core, core_send.at[1], core_recv.at[1], {"node": other})
     join.start()
     for n in range(width // 256):
         cols = slice(n * 256, (n + 1) * 256)
@@ -399,13 +400,11 @@
             total = total + part_in[i, :, cols].astype(F32)
         mixed[:, cols] = total.astype(BF)
     join.wait()
-    both = dots[...] + dots_core[...]
-    small = lax.broadcasted_iota(jnp.int32, (rows, top), 1)
-    grads = jnp.zeros((rows, top), F32)
+    both = dots_sum[...] + dots_core[...]
     for k in range(top):
-        one = jnp.sum(jnp.where(ids[:, k:k + 1] == lane, both, 0.0), axis=1, keepdims=True)
-        grads = jnp.where(small == k, one, grads)
-    gate_grad[...] = grads
+        gate_grad[k:k + 1, :] = jnp.sum(
+            jnp.where(ids[k:k + 1, :] == expert_row, both, 0.0), axis=0, keepdims=True
+        )
 
     for s in range(levels):
         spread_done(s)
@@ -432,18 +431,18 @@
     vm = pl.BlockSpec(memory_space=pltpu.VMEM)
     hbm = pl.BlockSpec(memory_space=pl.ANY)
     dma = pltpu.SemaphoreType.DMA
-    return pl.pallas_call(
+    mixed, gate_grad = pl.pallas_call(
         layer_kernel,
         out_shape=(
             jax.ShapeDtypeStruct((rows, width), BF),
-            jax.ShapeDtypeStruct((rows, top), F32),
+            jax.ShapeDtypeStruct((top, rows), F32),
         ),
         in_specs=[hbm, vm, vm, hbm, hbm, hbm, vm, vm, hbm, hbm],
         out_specs=(vm, vm),
         scratch_shapes=[
             pltpu.VMEM((levels, rows, width), BF),
             pltpu.VMEM((levels, rows, width), BF),
-            pltpu.VMEM((levels, 2 * rows + experts, 128), F32),
+            pltpu.VMEM((levels, 2 * experts, rows), F32),
             pltpu.VMEM((width, 2 * inner), BF),
             pltpu.VMEM((width, 2 * inner), BF),
             pltpu.VMEM((2 * inner, width), BF),
@@ -459,10 +458,12 @@
             pltpu.VMEM((rows, width), F32),
             pltpu.VMEM((levels, rows, width), BF),
             pltpu.VMEM((levels, rows, width), BF),
-            pltpu.VMEM((levels, rows, 128), F32),
-            pltpu.VMEM((levels, rows, 128), F32),
+            pltpu.VMEM((levels, experts, rows), F32),
+            pltpu.VMEM((levels, experts, rows), F32),
             pltpu.VMEM((rows, 128), F32),
             pltpu.VMEM((rows, 128), F32),
+            pltpu.VMEM((experts, rows), F32),
+            pltpu.VMEM((experts, rows), F32),
             dma((6,)),
             dma((2,)),
             dma((levels,)),
@@ -485,9 +486,10 @@
             collective_id=0, has_side_effects=True, vmem_limit_bytes=58 * 1024 * 1024
         ),
     )(
-        tokens, expert_ids, gate_probs, w_gate, w_up, w_down, gate_scale, up_scale, down_scale,
+        tokens, expert_ids.T, gate_probs.T, w_gate, w_up, w_down, gate_scale, up_scale, down_scale,
         cotangent,
     )
+    return mixed, gate_grad.T
 
 
 def solution(mesh):

time: 153 us -> 123 us (0.80)
  Pallas kernels: 144 us -> 117 us
  local copies, waits for them, and re-layouts: 6.14 us -> 3.09 us
    pallas_call x1, Pallas kernels: 144 us -> 117 us  [fused(): pl.pallas_call(layer_kernel, out_shape=(jax.ShapeDtypeStruct((rows, width...]
    unnamed x3 -> x2, local copies, waits for them, and re-layouts: 4.64 us -> 3.09 us
where the time goes in v3:
time: 123 us; the launch traced here: 121 us
  Pallas kernels  117 us (95%)
  local copies, waits for them, and re-layouts  3.09 us (3%)
    pallas_call x1, Pallas kernels, fused(): pl.pallas_call(layer_kernel, out_shape=(jax.ShapeDtypeStruct((rows, width...  117 us
    unnamed x2, local copies, waits for them, and re-layouts  3.09 us

profile of v3, /device:TPU:27, one launch (start us, length us, event | category | flops | bytes accessed | tf_op | source)
XLA Modules:
  0.0 121.2 jit_solution(14878848679903689224)
XLA Ops:
  0.6 117.5 %shard_map.113 = (bf16[128,1792]{1,0:T(8,128)(2,1)}, f32[8,128]{1,0:T(8,128)}) custom-call(bf16[128,1792]{1,0:T(8,128)(2,1)} %tokens.1, s32[8,128]{1,0:T(8,128)} %bitcast.3, f32[8,128]{1,0:T(8,128)} %bitcast.4, bf16[1,1792,1024]{2,1,0:T(8,128)(2,1)} %w_gate.1, bf16[1,1792,1024]{2,1,0:T(8,128)(2,1)} %w_up.1, bf16[1,512,3584]{2,1,0:T(8,128)(2,1)} %w_down.1, ...), custom_call_target="tpu_custom_call" | custom-call | tf_op jit(solution)/shard_map/pallas_call | solution.py:434
  118.1 1.8 %copy.14 = bf16[128,1792]{1,0:T(8,128)(2,1)} copy(bf16[128,1792]{1,0:T(8,128)(2,1)} %get-tuple-element.8) | data formatting | bytes 917504
  119.9 1.3 %copy.15 = f32[128,8]{0,1:T(8,128)} copy(f32[128,8]{0,1:T(8,128)} %bitcast.5) | data formatting | bytes 8192
